TPU v7x, 768 devices: a whole 4x8x12 slice. The times are simulated.
768 devices in a mesh: rows: 64 (over y, x, core), grp: 12 (over z).
Axes of the slice: x: 4, y: 8, z: 12, core: 2. Of those that a mesh axis runs over, the one named last changes fastest.
Arguments:
- points: float32 [196608, 440], P(('rows', 'grp')), may hold values from -5 to 5
- targets: float32 [196608, 147], P(('rows', 'grp')), may hold values from -6 to 6
- coefs_start: float32 [196608, 147], P(('rows', 'grp')), may hold values from -0.6 to 0.6
- block_index: int32 [3, 256], replicated, may hold values from 0 to 196607, as said below
Outputs:
- coefficients: float32 [196608, 147], P(('rows', 'grp'))
Inputs may be any that keep to these rules, and one draw needn't show every extreme that they name: `block_index`: devices of the rows+grp axis are numbered r * 12 + g, and device d holds rows d * 256 to (d + 1) * 256 - 1. For each block, entries r * 4 to (r + 1) * 4 - 1 are distinct rows held by device (r, g) for one grp index g of that block, the same g for all r. Different blocks may share rows. Block 0 holds row 0 and block 1 holds row 196607.
All inputs are finite; a program needn't handle non-finite values.
Results may differ from a plain program's by a relative error of at most 0.0003.
Values sent between devices are 32-bit elements; how exact they have to be, the bound alone decides.
A program may use at most 32 MiB of HBM per device.

v0:
```python
import jax
import jax.numpy as jnp
from jax import lax
from jax.sharding import PartitionSpec as P

ridge = 0.5


def broadcast(block, axis, holder):
    block = jnp.where(lax.axis_index(axis) == holder, block, jnp.zeros_like(block))
    return lax.psum(block, axis)


def kernel(left, right):
    left_sq = jnp.sum(left * left, axis=1)
    right_sq = jnp.sum(right * right, axis=1)
    cross = jnp.dot(
        left, right.T, precision=lax.Precision.HIGHEST, preferred_element_type=jnp.float32
    )
    dist = left_sq[:, None] + right_sq[None, :] - 2.0 * cross
    return jnp.exp(-2.0 * dist / points_width(left))


def points_width(left):
    return float(left.shape[1])


def locate(index_row, local_rows):
    part_rows = index_row.shape[0] // lax.axis_size("rows")
    my_line = lax.axis_index("rows")
    mine = lax.dynamic_slice_in_dim(index_row, my_line * part_rows, part_rows)
    offsets = mine % local_rows
    holder = index_row[0] // local_rows % lax.axis_size("grp")
    return (offsets, holder, my_line, part_rows)


def collect(points, targets, coefficients, index_row):
    offsets, holder, my_line, part_rows = locate(index_row, points.shape[0])
    picked = jnp.concatenate([points[offsets], targets[offsets], coefficients[offsets]], axis=1)
    spread = broadcast(picked, "grp", holder)
    arrived = lax.all_gather(spread, "rows", axis=0, tiled=True)
    width = points.shape[1]
    classes = targets.shape[1]
    return (arrived[:, :width], arrived[:, width : width + classes], arrived[:, width + classes :])


def place(coefficients, change, index_row):
    offsets, holder, my_line, part_rows = locate(index_row, coefficients.shape[0])
    my_change = lax.dynamic_slice_in_dim(change, my_line * part_rows, part_rows)
    update = jnp.where(lax.axis_index("grp") == holder, my_change, jnp.zeros_like(my_change))
    return coefficients.at[offsets].add(update)


def solve_block(kern_block, right_side):
    system = kern_block + ridge * jnp.eye(kern_block.shape[0], dtype=jnp.float32)
    factor = jnp.linalg.cholesky(system)
    return jax.scipy.linalg.cho_solve((factor, True), right_side)


def local_term(block_points, points, coefficients):
    return jnp.dot(
        kernel(block_points, points),
        coefficients,
        precision=lax.Precision.HIGHEST,
        preferred_element_type=jnp.float32,
    )


def body(points, targets, coefs_start, block_index):
    coefficients = coefs_start
    count = block_index.shape[0]
    for current in range(count):
        block_points, block_targets, block_coefs = collect(
            points, targets, coefficients, block_index[current]
        )
        partial_value = local_term(block_points, points, coefficients)
        summed = lax.psum(partial_value, ("rows", "grp"))
        change = solve_block(
            kernel(block_points, block_points), block_targets - ridge * block_coefs - summed
        )
        coefficients = place(coefficients, change, block_index[current])
    return coefficients


def solution(mesh):
    return jax.shard_map(
        body,
        mesh=mesh,
        in_specs=(
            P(("rows", "grp"), None),
            P(("rows", "grp"), None),
            P(("rows", "grp"), None),
            P(),
        ),
        out_specs=P(("rows", "grp"), None),
        check_vma=False,
    )
```

profile of v0, /device:TPU:1, one launch (start us, length us, event | category | flops | bytes accessed | tf_op | source)
XLA Modules:
  0.0 1668.5 jit_solution(3728179400685976674)
XLA Ops:
  6.5 0.7 copy-done.3
  10.4 1.1 multiply_reduce_fusion.3
  12.5 0.8 copy-done.1
  15.2 42.7 %psum.42 = f32[4,734]{1,0:T(4,128)S(1)} all-reduce(f32[4,734]{1,0:T(4,128)S(1)} %maximum_select_fusion), channel_id=1, replica_groups=mesh['rows'=64,'grp'=12] {'grp'}, use_global_device_ids=true, to_apply=%region_0.1 | all-reduce | flops 2936 | bytes 23488 | tf_op jit(solution)/shard_map/psum | solution.py:11
  58.0 62.3 %all-gather = f32[64,4,734]{2,1,0:T(4,128)S(1)} all-gather(f32[1,4,734]{2,1,0:T(4,128)S(1)} %bitcast.141), channel_id=1, replica_groups=mesh['rows'=64,'grp'=12] {'rows'}, dimensions={0}, use_global_device_ids=true | all-gather | bytes 763360 | tf_op jit(solution)/shard_map/all_gather | solution.py:41
  120.7 1.0 fusion.6
  121.7 1.0 fusion.83
  130.1 11.7 cholesky.172
  142.5 9.8 custom-call.17
  152.9 11.7 cholesky.189
  166.6 4.3 while.6
  167.6 1.3 bitcast_dynamic-update-slice_fusion.6
  169.5 1.3 bitcast_dynamic-update-slice_fusion.6
  172.2 19.7 %custom-call.18 = f32[2,128,128]{1,2,0:T(8,128)S(1)} custom-call(f32[2,128,128]{2,1,0:T(8,128)S(1)} %get-tuple-element.27), custom_call_target="InvertDiagBlocksLowerTriangular" | custom-call | tf_op jit(solution)/shard_map/jit(_cho_solve)/triangular_solve | solution.py:57
  191.9 375.4 %all-reduce.5.cloned.1.call-done = f32[256,147]{0,1:T(8,128)} async-done(((f32[256,147]{0,1:T(8,128)}), f32[256,147]{0,1:T(8,128)}) %all-reduce.5.cloned.1.call-update) | async-done | bytes 150544 | tf_op jit(solution)/shard_map/psum | solution.py:77
  567.3 1.0 subtract_subtract_fusion.2
  570.2 0.8 scatter_fusion
  571.6 31.1 %psum.44 = f32[4,734]{1,0:T(4,128)S(1)} all-reduce(f32[4,734]{1,0:T(4,128)S(1)} %maximum_select_fusion.1), channel_id=1, replica_groups=mesh['rows'=64,'grp'=12] {'grp'}, use_global_device_ids=true, to_apply=%region_9.12 | all-reduce | flops 2936 | bytes 23488 | tf_op jit(solution)/shard_map/psum | solution.py:11
  602.7 59.7 %all-gather.1 = f32[64,4,734]{2,1,0:T(4,128)S(1)} all-gather(f32[1,4,734]{2,1,0:T(4,128)S(1)} %bitcast.142), channel_id=1, replica_groups=mesh['rows'=64,'grp'=12] {'rows'}, dimensions={0}, use_global_device_ids=true | all-gather | bytes 763360 | tf_op jit(solution)/shard_map/all_gather | solution.py:41
  663.5 1.0 fusion.13
  664.5 1.2 fusion.84
  666.2 11.7 cholesky.206
  677.9 0.7 compare_reduce_fusion.3
  678.6 9.8 custom-call.19
  688.9 11.7 cholesky.223
  702.7 4.1 while.7
  703.4 1.3 bitcast_dynamic-update-slice_fusion.7
  705.4 1.3 bitcast_dynamic-update-slice_fusion.7
  707.2 19.7 %custom-call.20 = f32[2,128,128]{1,2,0:T(8,128)S(1)} custom-call(f32[2,128,128]{2,1,0:T(8,128)S(1)} %get-tuple-element.28), custom_call_target="InvertDiagBlocksLowerTriangular" | custom-call | tf_op jit(solution)/shard_map/jit(_cho_solve)/triangular_solve | solution.py:57
  726.8 385.2 %all-reduce.7.cloned.1.call-done = f32[256,147]{0,1:T(8,128)} async-done(((f32[256,147]{0,1:T(8,128)}), f32[256,147]{0,1:T(8,128)}) %all-reduce.7.cloned.1.call-update) | async-done | bytes 150544 | tf_op jit(solution)/shard_map/psum | solution.py:77
  1112.0 1.0 subtract_subtract_fusion.1
  1114.9 0.8 scatter_fusion.1
  1116.4 31.1 %psum.46 = f32[4,734]{1,0:T(4,128)S(1)} all-reduce(f32[4,734]{1,0:T(4,128)S(1)} %maximum_select_fusion.2), channel_id=1, replica_groups=mesh['rows'=64,'grp'=12] {'grp'}, use_global_device_ids=true, to_apply=%region_13.16 | all-reduce | flops 2936 | bytes 23488 | tf_op jit(solution)/shard_map/psum | solution.py:11
  1147.5 59.9 %all-gather.2 = f32[64,4,734]{2,1,0:T(4,128)S(1)} all-gather(f32[1,4,734]{2,1,0:T(4,128)S(1)} %bitcast.143), channel_id=1, replica_groups=mesh['rows'=64,'grp'=12] {'rows'}, dimensions={0}, use_global_device_ids=true | all-gather | bytes 763360 | tf_op jit(solution)/shard_map/all_gather | solution.py:41
  1207.8 1.0 fusion.20
  1209.5 1.2 fusion.85
  1210.9 11.7 cholesky.240
  1223.3 9.8 custom-call.21
  1233.6 12.0 cholesky.257
  1245.6 0.7 compare_reduce_fusion
  1247.7 4.0 while.8
  1248.3 1.3 bitcast_dynamic-update-slice_fusion.8
  1250.3 1.3 bitcast_dynamic-update-slice_fusion.8
  1252.1 19.7 %custom-call.22 = f32[2,128,128]{1,2,0:T(8,128)S(1)} custom-call(f32[2,128,128]{2,1,0:T(8,128)S(1)} %get-tuple-element.29), custom_call_target="InvertDiagBlocksLowerTriangular" | custom-call | tf_op jit(solution)/shard_map/jit(_cho_solve)/triangular_solve | solution.py:57
  1271.7 385.3 %all-reduce.9.cloned.1.call-done = f32[256,147]{0,1:T(8,128)} async-done(((f32[256,147]{0,1:T(8,128)}), f32[256,147]{0,1:T(8,128)}) %all-reduce.9.cloned.1.call-update) | async-done | bytes 150544 | tf_op jit(solution)/shard_map/psum | solution.py:77
  1657.1 1.0 subtract_subtract_fusion
  1660.0 0.8 scatter_fusion.2
  1660.8 0.8 copy.73
  (124 shorter events, 26.5 us)
Async XLA Ops:
  6.5 0.7 copy-start.3
  6.5 5.0 copy-start
  6.5 560.7 %all-reduce.5.cloned.1.call-start = ((), (), s32[]{:S(2)}) async-start(), calls=%async_computation | async-start | bytes 311296 | tf_op jit(solution)/shard_map/psum | solution.py:77
  11.5 0.9 copy-start.2
  12.4 0.9 copy-start.1
  122.7 989.3 %all-reduce.7.cloned.1.call-start = ((), (), s32[]{:S(2)}) async-start(), calls=%async_computation.1 | async-start | bytes 311296 | tf_op jit(solution)/shard_map/psum | solution.py:77
  665.8 991.3 %all-reduce.9.cloned.1.call-start = ((), (), s32[]{:S(2)}) async-start(), calls=%async_computation.2 | async-start | bytes 311296 | tf_op jit(solution)/shard_map/psum | solution.py:77
Sparse Core Ops, SparseCore 0:
  122.9 444.3 all-reduce.4
  665.9 446.1 all-reduce.6
  1210.8 446.1 all-reduce.8
where the time goes:
time: 1670 us
  waiting for transfers between devices  1150 us (69%)
  blocking collectives  287 us (17%)
  other arithmetic  171 us (10%)
  between operations  25.4 us (2%)
  local copies, waits for them, and re-layouts  23.4 us (1%)
    psum x3, waiting for transfers between devices, body(): summed = lax.psum(partial_value, ('rows', 'grp'))  1150 us
    all_gather x3, blocking collectives, collect(): arrived = lax.all_gather(spread, 'rows', axis=0, tiled=True)  182 us
    psum x3, blocking collectives, broadcast(): return lax.psum(block, axis)  105 us
    another operation x21, other arithmetic, solve_block(): factor = jnp.linalg.cholesky(system)  104 us
    another operation x7, other arithmetic, solve_block(): return jax.scipy.linalg.cho_solve((factor, True), right_side)  59.1 us
  transfers between devices with their start and end apart: 3, of which 3 were waited for; matrix products, arithmetic and copies ran while one was open for 11% of the time, Pallas kernels for 0%

commit v1 on v0

v1 whole, which is shorter than its diff:
```python
import functools

import jax
import jax.numpy as jnp
from jax import lax
from jax.experimental import pallas as pl
from jax.experimental.pallas import tpu as pltpu
from jax.sharding import PartitionSpec as P

HIGH = lax.Precision.HIGHEST
VMEM = pl.BlockSpec(memory_space=pltpu.VMEM)
SMEM = pl.BlockSpec(memory_space=pltpu.SMEM)
MESH = pl.DeviceIdType.MESH
NY, NX, NC, NZ = 8, 4, 2, 12
PART = 4
CHUNKS = 4
PAD = 512
ridge = 0.5


def dot(a, b, ca=1, cb=0):
    return lax.dot_general(a, b, (((ca,), (cb,)), ((), ())), precision=HIGH, preferred_element_type=jnp.float32)


def row_of(v, k):
    return jnp.broadcast_to(v[k:k + 1, :], v.shape)


def lane_of(v, k):
    return jnp.broadcast_to(v[:, k:k + 1], v.shape)


def eliminate(rows, t):
    place = lax.broadcasted_iota(jnp.int32, (8, 128), 0)
    top = rows[0]
    spread = [[lane_of(v, j) for j in range(8)] for v in rows[1:]]
    cols = [lane_of(top, j) for j in range(8)]
    forward = top
    full = top
    scale = jnp.zeros((8, 128), jnp.float32)
    for k in range(8):
        pivot = row_of(cols[k], k)
        inverse = 1.0 / pivot
        scale = jnp.where(place == k, inverse, scale)
        step = cols[k] * inverse
        both = jnp.where(place == k, 0.0, step)
        below = jnp.where(place > k, step, 0.0)
        for j in range(k + 1, 8):
            cols[j] = cols[j] - both * row_of(cols[j], k)
        forward = forward - below * row_of(forward, k)
        full = full - both * row_of(full, k)
    solved = full * scale
    done = forward * jnp.sqrt(scale)
    lines = [row_of(solved, j) for j in range(8)]
    out = []
    for p in range(1, 8):
        s = spread[p - 1]
        terms = [s[j] * lines[j] for j in range(8)]
        total = ((terms[0] + terms[1]) + (terms[2] + terms[3])) + ((terms[4] + terms[5]) + (terms[6] + terms[7]))
        live = jnp.where(t + p < 8, 1.0, 0.0).astype(jnp.float32)
        out.append(rows[p] - live * total)
    out.append(done)
    return [pltpu.roll(v, 120, 1) for v in out]


def factor64(blocks):
    n = len(blocks)
    unit = (lax.broadcasted_iota(jnp.int32, (64, 64), 0) == lax.broadcasted_iota(jnp.int32, (64, 64), 1)).astype(jnp.float32)
    state = []
    for b in blocks:
        w = jnp.concatenate([b, unit], axis=1)
        state += [w[8 * p:8 * p + 8, :] for p in range(8)]
    def group(t, state):
        out = []
        for m in range(n):
            out += eliminate(list(state[8 * m:8 * m + 8]), t)
        return tuple(out)
    state = lax.fori_loop(0, 8, group, tuple(state))
    return [jnp.concatenate(state[8 * m:8 * m + 8], axis=0)[:, :64] for m in range(n)]


def factor256(work):
    n = work.shape[0]
    for j in range(4):
        lo, hi = 64 * j, 64 * j + 64
        invs = factor64([work[m, lo:hi, lo:hi] for m in range(n)])
        for m in range(n):
            rows = dot(invs[m], work[m, lo:hi, :])
            work[m, lo:hi, :] = rows
            if j < 3:
                work[m, hi:, :] = work[m, hi:, :] - dot(rows[:, hi:256], rows, 0, 0)


def iota(shape, axis):
    return lax.broadcasted_iota(jnp.int32, shape, axis)


def spot():
    line = lax.axis_index("rows")
    return line // (NX * NC), line // NC % NX, line % NC, lax.axis_index("grp")


def device(y, x, c, z):
    return ((y * NX + x) * NC + c, z)


def partner(axis, step):
    y, x, c, z = spot()
    if axis == "y":
        return device((y + step) % NY, x, c, z)
    if axis == "x":
        return device(y, (x + step) % NX, c, z)
    if axis == "z":
        return device(y, x, c, (z + step) % NZ)
    return device(y, x, (c + step) % NC, z)


SIZES = {"y": NY, "x": NX, "z": NZ, "c": NC}


def greet():
    barrier = pltpu.get_barrier_semaphore()
    count = 0
    for axis, size in SIZES.items():
        for step in range(1, size):
            pl.semaphore_signal(barrier, inc=1, device_id=partner(axis, step), device_id_type=MESH)
            count += 1
    pl.semaphore_wait(barrier, count)


class Mail:
    def __init__(self, send_sem, recv_sem):
        self.send_sem, self.recv_sem, self.used, self.sent = send_sem, recv_sem, 0, []

    def send(self, axis, step, source, target):
        copy = pltpu.make_async_remote_copy(
            src_ref=source,
            dst_ref=target,
            send_sem=self.send_sem.at[self.used],
            recv_sem=self.recv_sem.at[self.used],
            device_id=partner(axis, step),
            device_id_type=MESH,
        )
        copy.start()
        self.used += 1
        self.sent.append(copy)
        return copy

    def spread(self, axis, source, target):
        return [self.send(axis, step, source, target) for step in range(1, SIZES[axis])]

    def close(self):
        for copy in self.sent:
            copy.wait_send()


def arrive(copies):
    for copy in copies:
        copy.wait_recv()


COPIES_GATHER = 2 * (NZ - 1) + (NX - 1) + (NY - 1) + (NX - 1) + (NY - 1) + (NX - 1) + (NY - 1) + (NZ - 1) + 1


def gather_body(points_ref, index_ref, out_ref, picked, landed, send_sem, recv_sem):
    y, x, c, z = spot()
    me = lax.axis_index("rows") * NZ + z
    line = lax.axis_index("rows")
    count, width = points_ref.shape
    mail = Mail(send_sem, recv_sem)
    blocks = index_ref.shape[0]
    picked[...] = jnp.zeros_like(picked)
    for k in range(blocks):
        for i in range(PART):
            row = index_ref[k, line * PART + i]
            mine = row // count == me
            value = points_ref[pl.ds(row % count, 1), :]
            value = jnp.where(mine, value, 0.0)
            for ch in range(CHUNKS):
                lo, hi = 128 * ch, min(128 * ch + 128, width)
                picked[PART * k + i, ch : ch + 1, : hi - lo] = value[:, lo:hi]
    greet()
    k, i = z // PART, z % PART
    step1 = [mail.send("z", s, picked.at[(z + s) % NZ], landed.at[s]) for s in range(1, NZ)]
    arrive(step1)
    row = picked[z]
    for s in range(1, NZ):
        row = row + landed[s]
    for ch in range(CHUNKS):
        out_ref[c, ch, x, k, y, pl.ds(i, 1), :] = row[ch : ch + 1, :]
    one = out_ref.at[c, 0:3, x, k, y, pl.ds(i, 1)]
    ab1 = mail.spread("z", one, one)
    one = out_ref.at[c, 3, x, k, y, pl.ds(i, 1)]
    c1 = mail.spread("x", one, one)
    arrive(c1)
    some = out_ref.at[c, 3, :, k, y, pl.ds(i, 1)]
    c2 = mail.spread("y", some, some)
    arrive(ab1)
    some = out_ref.at[c, 0:2, x, :, y]
    a2 = mail.spread("y", some, some)
    some = out_ref.at[c, 2, x, :, y]
    b2 = mail.spread("x", some, some)
    arrive(c2)
    many = out_ref.at[c, 3, :, k, :, pl.ds(i, 1)]
    c3 = mail.spread("z", many, many)
    arrive(b2)
    many = out_ref.at[c, 2, :, :, y]
    b3 = mail.spread("y", many, many)
    arrive(a2)
    many = out_ref.at[c, 0:2, x]
    a3 = mail.spread("x", many, many)
    arrive(a3)
    arrive(b3)
    arrive(c3)
    last = [mail.send("c", 1, out_ref.at[c], out_ref.at[c])]
    arrive(last)
    mail.close()


def squares(rows):
    return dot(jnp.ones((8, rows.shape[1]), jnp.float32), rows * rows, 1, 1)[:1]


def kernel_block(left, right, width):
    cross = sum(dot(a, b, 1, 1) for a, b in zip(left, right))
    left_sq = sum(jnp.sum(a * a, axis=1, keepdims=True) for a in left)
    right_sq = sum(squares(b) for b in right)
    return jnp.exp((left_sq + right_sq - 2.0 * cross) * (-2.0 / width))


def block_chunks(block_ref, k):
    return [jnp.concatenate([block_ref[c, ch, :, k].reshape(-1, 128) for c in range(NC)]) for ch in range(CHUNKS)]


def partial_body(block_ref, points_ref, targets_ref, coefs_ref, index_ref, out_ref, work):
    me = lax.axis_index("rows") * NZ + lax.axis_index("grp")
    coefs = coefs_ref[...]
    count, width = points_ref.shape
    classes = coefs.shape[1]
    start = targets_ref[...] - ridge * coefs
    work[...] = jnp.zeros_like(work)
    work[:, :width] = points_ref[...]
    points = [work[:, 128 * ch : 128 * ch + 128] for ch in range(CHUNKS)]
    out_ref[...] = jnp.zeros_like(out_ref)
    for k in range(block_ref.shape[3]):
        kern = kernel_block(points, block_chunks(block_ref, k), width)
        here = index_ref[k : k + 1, :] == iota(kern.shape, 0) + me * count
        total = dot(coefs, kern, 0, 0) - dot(start, here.astype(jnp.float32), 0, 0)
        for c in range(NC):
            out_ref[c, 152 * k : 152 * k + classes, :] = total[:, 128 * c : 128 * c + 128]


def solve_body(block_ref, index_ref, out_ref, work):
    line = lax.axis_index("rows")
    width = 440
    n, size = work.shape[0], work.shape[1]
    unit = (iota((size, size), 0) == iota((size, size), 1)).astype(jnp.float32)
    parts = [block_chunks(block_ref, k) for k in range(n)]
    rows = [index_ref[k : k + 1, :].astype(jnp.float32) for k in range(n)]
    for k in range(n):
        work[k, :, :size] = kernel_block(parts[k], parts[k], width) + ridge * unit
        work[k, :, size:] = unit
    factor256(work)
    link = {}
    for k in range(1, n):
        column = jnp.sum(jnp.where(unit > 0.0, rows[k], 0.0), axis=1, keepdims=True)
        for j in range(k):
            same = (column == rows[j]).astype(jnp.float32)
            link[k, j] = kernel_block(parts[k], parts[j], width) + ridge * same
    y, x, c, z = spot()
    height = out_ref.shape[0]
    pick, lane = iota((height, size), 0), iota((height, size), 1)
    found = {}
    for k in reversed(range(n)):
        mine = (pick // PART == k) & (lane == ((c * NX + x) * NY + y) * PART + pick % PART)
        value = mine.astype(jnp.float32)
        for j in range(k + 1, n):
            value = value - dot(found[j], link[j, k])
        inverse = work[k, :, size:]
        found[k] = dot(dot(value, inverse, 1, 1), inverse)
        out_ref[:, size * k : size * (k + 1)] = found[k]


COPIES_TOTAL = 1 + (NX - 1) + (NY - 1) + (NZ - 1) + (NY - 1) + (NX - 1) + 1


def total_body(part_ref, out_ref, from_c, from_x, from_y, from_z, sum_c, sum_x, sum_y, send_sem, recv_sem):
    y, x, c, z = spot()
    mail = Mail(send_sem, recv_sem)
    tall, low = PAD // NX, PAD // NX // NY
    greet()
    arrive([mail.send("c", 1, part_ref.at[1 - c], from_c)])
    sum_c[...] = part_ref[c] + from_c[...]
    copies = []
    for s in range(1, NX):
        piece = sum_c.at[pl.ds(pl.multiple_of((x + s) % NX * tall, tall), tall)]
        copies.append(mail.send("x", s, piece, from_x.at[s]))
    arrive(copies)
    total = sum_c[pl.ds(pl.multiple_of(x * tall, tall), tall)]
    for s in range(1, NX):
        total = total + from_x[s]
    sum_x[...] = total
    copies = []
    for s in range(1, NY):
        piece = sum_x.at[pl.ds(pl.multiple_of((y + s) % NY * low, low), low)]
        copies.append(mail.send("y", s, piece, from_y.at[s]))
    arrive(copies)
    total = sum_x[pl.ds(pl.multiple_of(y * low, low), low)]
    for s in range(1, NY):
        total = total + from_y[s]
    sum_y[...] = total
    arrive([mail.send("z", s, sum_y, from_z.at[s]) for s in range(1, NZ)])
    for s in range(1, NZ):
        total = total + from_z[s]
    mine = pl.ds(pl.multiple_of(x * tall + y * low, low), low)
    out_ref[c, mine, :] = total
    arrive(mail.spread("y", out_ref.at[c, mine], out_ref.at[c, mine]))
    mine = pl.ds(pl.multiple_of(x * tall, tall), tall)
    arrive(mail.spread("x", out_ref.at[c, mine], out_ref.at[c, mine]))
    arrive([mail.send("c", 1, out_ref.at[c], out_ref.at[c])])
    mail.close()


def place_body(total_ref, rows_ref, coefs_ref, index_ref, out_ref, change_ref):
    line = lax.axis_index("rows")
    me = line * NZ + lax.axis_index("grp")
    count, classes = coefs_ref.shape
    change = jnp.zeros(change_ref.shape, jnp.float32)
    for k in range(index_ref.shape[0]):
        for c in range(NC):
            at = 256 * k + 128 * c
            change = change - dot(rows_ref[:, at : at + 128], total_ref[c, 152 * k : 152 * k + classes, :], 1, 1)
    change_ref[...] = change
    out_ref[...] = coefs_ref[...]
    for k in range(index_ref.shape[0]):
        for i in range(PART):
            row = index_ref[k, line * PART + i]
            mine = jnp.where(row // count == me, 1.0, 0.0).astype(jnp.float32)
            at = pl.ds(row % count, 1)
            out_ref[at, :] = out_ref[at, :] + mine * change_ref[pl.ds(PART * k + i, 1), :]


def body(points, targets, coefs, block_index):
    blocks, size = block_index.shape
    count, width = points.shape
    classes = targets.shape[1]
    order = block_index.reshape(blocks, NY, NX, NC, PART).transpose(0, 3, 2, 1, 4).reshape(blocks, size)
    params = pltpu.CompilerParams(vmem_limit_bytes=40 << 20)
    f32 = jnp.float32
    arrived = pl.pallas_call(
        gather_body,
        out_shape=jax.ShapeDtypeStruct((NC, CHUNKS, NX, blocks, NY, PART, 128), f32),
        in_specs=[VMEM, SMEM],
        out_specs=VMEM,
        scratch_shapes=[
            pltpu.VMEM((NZ, CHUNKS, 128), f32),
            pltpu.VMEM((NZ, CHUNKS, 128), f32),
            pltpu.SemaphoreType.DMA((COPIES_GATHER,)),
            pltpu.SemaphoreType.DMA((COPIES_GATHER,)),
        ],
        compiler_params=pltpu.CompilerParams(vmem_limit_bytes=40 << 20, collective_id=1, has_side_effects=True),
        name="gather_blocks",
    )(points, block_index)
    arrived = arrived.reshape(NC, CHUNKS, NX, blocks, NY * PART, 128)
    partial_value = pl.pallas_call(
        partial_body,
        out_shape=jax.ShapeDtypeStruct((NC, PAD, 128), f32),
        in_specs=[VMEM] * 5,
        out_specs=VMEM,
        scratch_shapes=[pltpu.VMEM((count, 128 * CHUNKS), f32)],
        compiler_params=params,
        name="partial_sums",
    )(arrived, points, targets, coefs, order)
    total = pl.pallas_call(
        total_body,
        out_shape=jax.ShapeDtypeStruct((NC, PAD, 128), f32),
        in_specs=[VMEM],
        out_specs=VMEM,
        scratch_shapes=[
            pltpu.VMEM((PAD, 128), f32),
            pltpu.VMEM((NX, PAD // NX, 128), f32),
            pltpu.VMEM((NY, PAD // NX // NY, 128), f32),
            pltpu.VMEM((NZ, PAD // NX // NY, 128), f32),
            pltpu.VMEM((PAD, 128), f32),
            pltpu.VMEM((PAD // NX, 128), f32),
            pltpu.VMEM((PAD // NX // NY, 128), f32),
            pltpu.SemaphoreType.DMA((COPIES_TOTAL,)),
            pltpu.SemaphoreType.DMA((COPIES_TOTAL,)),
        ],
        compiler_params=pltpu.CompilerParams(vmem_limit_bytes=40 << 20, collective_id=2, has_side_effects=True),
        name="total_sums",
    )(partial_value)
    rows = pl.pallas_call(
        solve_body,
        out_shape=jax.ShapeDtypeStruct((16, blocks * size), f32),
        in_specs=[VMEM] * 2,
        out_specs=VMEM,
        scratch_shapes=[pltpu.VMEM((blocks, size, 2 * size), f32)],
        compiler_params=params,
        name="solve_rows",
    )(arrived, order)
    return pl.pallas_call(
        place_body,
        out_shape=jax.ShapeDtypeStruct(coefs.shape, f32),
        in_specs=[VMEM, VMEM, VMEM, SMEM],
        out_specs=VMEM,
        scratch_shapes=[pltpu.VMEM((16, classes), f32)],
        compiler_params=params,
        name="place_change",
    )(total, rows, coefs, block_index)


def solution(mesh):
    return jax.shard_map(
        body,
        mesh=mesh,
        in_specs=(
            P(("rows", "grp"), None),
            P(("rows", "grp"), None),
            P(("rows", "grp"), None),
            P(),
        ),
        out_specs=P(("rows", "grp"), None),
        check_vma=False,
    )
```

time: 1670 us -> 141 us (0.08)
  waiting for transfers between devices: 1150 us -> 0 us
  blocking collectives: 287 us -> 0 us
  other arithmetic: 171 us -> 0 us
  Pallas kernels: 0 us -> 135 us
  between operations: 25.4 us -> 0.08 us
  local copies, waits for them, and re-layouts: 23.4 us -> 5.15 us
    psum x3 -> x0, waiting for transfers between devices: 1150 us -> none  [body(): summed = lax.psum(partial_value, ('rows', 'grp'))]
    all_gather x3 -> x0, blocking collectives: 182 us -> none  [collect(): arrived = lax.all_gather(spread, 'rows', axis=0, tiled=True)]
    another operation x28 -> x0, other arithmetic: 163 us -> none  [the longest x21 104 us: solve_block(): factor = jnp.linalg.cholesky(system)]
    pallas_call x0 -> x5, Pallas kernels: none -> 135 us  [the longest x1 48.3 us: body(): pl.pallas_call(gather_body, out_shape=jax.ShapeDtypeStruct((NC, CHUNKS, N...]
    psum x3 -> x0, blocking collectives: 105 us -> none  [broadcast(): return lax.psum(block, axis)]
  transfers between devices with their start and end apart: 3 -> 0, of which waited for: 3 -> 0; matrix products, arithmetic and copies ran while one was open for 11% -> 0% of each run, Pallas kernels for 0% -> 0%
where the time goes in v1:
time: 141 us; the launch traced here: 140 us
  Pallas kernels  135 us (96%)
  local copies, waits for them, and re-layouts  5.15 us (4%)
    pallas_call x1, Pallas kernels, body(): pl.pallas_call(gather_body, out_shape=jax.ShapeDtypeStruct((NC, CHUNKS, N...  48.3 us
    pallas_call x1, Pallas kernels, body(): pl.pallas_call(solve_body, out_shape=jax.ShapeDtypeStruct((16, blocks * s...  42.6 us
    pallas_call x1, Pallas kernels, body(): pl.pallas_call(total_body, out_shape=jax.ShapeDtypeStruct((NC, PAD, 128),...  35.9 us
    pallas_call x1, Pallas kernels, body(): pl.pallas_call(partial_body, out_shape=jax.ShapeDtypeStruct((NC, PAD, 128...  6.93 us
    unnamed x5, local copies, waits for them, and re-layouts  3.3 us

profile of v1, /device:TPU:1, one launch (start us, length us, event | category | flops | bytes accessed | tf_op | source)
XLA Modules:
  0.0 140.4 jit_solution(18436029374674683371)
XLA Ops:
  0.0 0.0 copy-start
  0.0 0.9 reshape.10
  1.0 0.1 reshape.11.index_ref
  1.1 1.0 copy.16.coefs_ref
  2.1 1.0 copy.15.targets_ref
  3.2 1.2 copy.12.points_ref
  4.4 0.0 copy-done
  4.4 48.3 %gather_blocks.1 = f32[2,4,4,3,8,4,128]{6,5,4,3,2,1,0:T(4,128)S(1)} custom-call(f32[256,440]{1,0:T(8,128)S(1)} %copy.12.points_ref, s32[3,256]{1,0:T(4,128)S(1)} %copy-done), custom_call_target="tpu_custom_call" | custom-call | tf_op jit(solution)/shard_map/gather_blocks/pallas_call | solution.py:350
  52.7 6.9 %partial_sums.1.part_ref = f32[2,512,128]{2,1,0:T(8,128)S(1)} custom-call(f32[2,4,4,3,32,128]{5,4,3,2,1,0:T(8,128)S(1)} %bitcast.4, f32[256,440]{1,0:T(8,128)S(1)} %copy.12.points_ref, f32[256,147]{1,0:T(8,128)S(1)} %copy.15.targets_ref, f32[256,147]{1,0:T(8,128)S(1)} %copy.16.coefs_ref, s32[3,256]{1,0:T(4,128)S(1)} %reshape.11.index_ref), custom_call_target="tpu_custom_call" | custom-call | tf_op jit(solution)/shard_map/partial_sums/pallas_call | solution.py:365
  59.7 42.6 %solve_rows.1.rows_ref = f32[16,768]{1,0:T(8,128)S(1)} custom-call(f32[2,4,4,3,32,128]{5,4,3,2,1,0:T(8,128)S(1)} %bitcast.5, s32[3,256]{1,0:T(4,128)S(1)} %reshape.11.index_ref), custom_call_target="tpu_custom_call" | custom-call | tf_op jit(solution)/shard_map/solve_rows/pallas_call | solution.py:393
  102.3 35.9 %total_sums.1.total_ref = f32[2,512,128]{2,1,0:T(8,128)S(1)} custom-call(f32[2,512,128]{2,1,0:T(8,128)S(1)} %partial_sums.1.part_ref), custom_call_target="tpu_custom_call" | custom-call | tf_op jit(solution)/shard_map/total_sums/pallas_call | solution.py:374
  138.2 1.5 %place_change.1 = f32[256,147]{1,0:T(8,128)S(1)} custom-call(f32[2,512,128]{2,1,0:T(8,128)S(1)} %total_sums.1.total_ref, f32[16,768]{1,0:T(8,128)S(1)} %solve_rows.1.rows_ref, f32[256,147]{1,0:T(8,128)S(1)} %copy.16.coefs_ref, s32[3,256]{1,0:T(4,128)S(1)} %copy-done), custom_call_target="tpu_custom_call" | custom-call | tf_op jit(solution)/shard_map/place_change/pallas_call | solution.py:402
  139.7 0.8 copy.18
  (1 shorter events, 0.0 us)
Async XLA Ops:
  0.0 4.4 %copy-start = (s32[3,256]{1,0:T(4,128)S(1)}, s32[3,256]{1,0:T(4,128)}, u32[]{:S(2)}) copy-start(s32[3,256]{1,0:T(4,128)} %index_ref.3) | copy-start | bytes 9220

commit v2 on v0

v2 whole, which is shorter than its diff:
```python
import functools

import jax
import jax.numpy as jnp
from jax import lax
from jax.experimental import pallas as pl
from jax.experimental.pallas import tpu as pltpu
from jax.sharding import PartitionSpec as P

HIGH = lax.Precision.HIGHEST
VMEM = pl.BlockSpec(memory_space=pltpu.VMEM)
SMEM = pl.BlockSpec(memory_space=pltpu.SMEM)
ANY = pl.BlockSpec(memory_space=pl.ANY)
MESH = pl.DeviceIdType.MESH
NY, NX, NC, NZ = 8, 4, 2, 12
PART = 4
CHUNKS = 4
PAD = 512
TALL, LOW = PAD // NX, PAD // NX // NY
CLASS_ROWS = 152
ROLES = 3
ridge = 0.5


def dot(a, b, ca=1, cb=0):
    return lax.dot_general(a, b, (((ca,), (cb,)), ((), ())), precision=HIGH, preferred_element_type=jnp.float32)


def row_of(v, k):
    return jnp.broadcast_to(v[k:k + 1, :], v.shape)


def lane_of(v, k):
    return jnp.broadcast_to(v[:, k:k + 1], v.shape)


def eliminate(rows, t):
    place = lax.broadcasted_iota(jnp.int32, (8, 128), 0)
    top = rows[0]
    spread = [[lane_of(v, j) for j in range(8)] for v in rows[1:]]
    cols = [lane_of(top, j) for j in range(8)]
    forward = top
    full = top
    scale = jnp.zeros((8, 128), jnp.float32)
    for k in range(8):
        pivot = row_of(cols[k], k)
        inverse = 1.0 / pivot
        scale = jnp.where(place == k, inverse, scale)
        step = cols[k] * inverse
        both = jnp.where(place == k, 0.0, step)
        below = jnp.where(place > k, step, 0.0)
        for j in range(k + 1, 8):
            cols[j] = cols[j] - both * row_of(cols[j], k)
        forward = forward - below * row_of(forward, k)
        full = full - both * row_of(full, k)
    solved = full * scale
    done = forward * jnp.sqrt(scale)
    lines = [row_of(solved, j) for j in range(8)]
    out = []
    for p in range(1, 8):
        s = spread[p - 1]
        terms = [s[j] * lines[j] for j in range(8)]
        total = ((terms[0] + terms[1]) + (terms[2] + terms[3])) + ((terms[4] + terms[5]) + (terms[6] + terms[7]))
        live = jnp.where(t + p < 8, 1.0, 0.0).astype(jnp.float32)
        out.append(rows[p] - live * total)
    out.append(done)
    return [pltpu.roll(v, 120, 1) for v in out]


def factor64(blocks):
    n = len(blocks)
    unit = (lax.broadcasted_iota(jnp.int32, (64, 64), 0) == lax.broadcasted_iota(jnp.int32, (64, 64), 1)).astype(jnp.float32)
    state = []
    for b in blocks:
        w = jnp.concatenate([b, unit], axis=1)
        state += [w[8 * p:8 * p + 8, :] for p in range(8)]
    def group(t, state):
        out = []
        for m in range(n):
            out += eliminate(list(state[8 * m:8 * m + 8]), t)
        return tuple(out)
    state = lax.fori_loop(0, 8, group, tuple(state))
    return [jnp.concatenate(state[8 * m:8 * m + 8], axis=0)[:, :64] for m in range(n)]


def iota(shape, axis):
    return lax.broadcasted_iota(jnp.int32, shape, axis)


def spot():
    line = lax.axis_index("rows")
    return line // (NX * NC), line // NC % NX, line % NC, lax.axis_index("grp")


def device(y, x, c, z):
    return ((y * NX + x) * NC + c, z)


def partner(axis, step):
    y, x, c, z = spot()
    if axis == "y":
        return device((y + step) % NY, x, c, z)
    if axis == "x":
        return device(y, (x + step) % NX, c, z)
    if axis == "z":
        return device(y, x, c, (z + step) % NZ)
    return device(y, x, (c + step) % NC, z)


SIZES = {"y": NY, "x": NX, "z": NZ, "c": NC}


def greet():
    barrier = pltpu.get_barrier_semaphore()
    count = 0
    for axis, size in SIZES.items():
        for step in range(1, size):
            pl.semaphore_signal(barrier, inc=1, device_id=partner(axis, step), device_id_type=MESH)
            count += 1
    return count


class Mail:
    def __init__(self, send_sem, recv_sem):
        self.send_sem, self.recv_sem, self.used, self.sent = send_sem, recv_sem, 0, []

    def send(self, axis, step, source, target):
        copy = pltpu.make_async_remote_copy(
            src_ref=source,
            dst_ref=target,
            send_sem=self.send_sem.at[self.used],
            recv_sem=self.recv_sem.at[self.used],
            device_id=partner(axis, step),
            device_id_type=MESH,
        )
        copy.start()
        self.used += 1
        self.sent.append(copy)
        return copy

    def spread(self, axis, source, target):
        return [self.send(axis, step, source, target) for step in range(1, SIZES[axis])]

    def close(self):
        for copy in self.sent:
            copy.wait_send()


def arrive(copies):
    for copy in copies:
        copy.wait_recv()


COPIES = (
    1 + 1 + 2 * (NZ - 1) + (NX - 1) + (NY - 1) + (NX - 1) + (NY - 1) + (NX - 1) + (NY - 1) + (NZ - 1) + 1
    + (NX - 1) + (NY - 1) + (NZ - 1) + (NY - 1) + (NX - 1) + 1
)


def half_rows(blocks_ref, c, k):
    return jnp.concatenate([blocks_ref[c, ch, :, k].reshape(-1, 128) for ch in range(CHUNKS)], axis=1)


def whole_rows(blocks_ref, k):
    return jnp.concatenate([half_rows(blocks_ref, c, k) for c in range(NC)], axis=0)


def kernel_block(left, right, width):
    cross = dot(left, right, 1, 1)
    left_sq = jnp.sum(left * left, axis=1, keepdims=True)
    right_sq = dot(jnp.ones((8, right.shape[1]), jnp.float32), right * right, 1, 1)[:1]
    return jnp.exp((left_sq + right_sq - 2.0 * cross) * (-2.0 / width))


def kernel_points(left, points, width):
    cross = dot(left, points, 1, 0)
    left_sq = jnp.sum(left * left, axis=1, keepdims=True)
    right_sq = jnp.sum(points * points, axis=0, keepdims=True)
    return jnp.exp((left_sq + right_sq - 2.0 * cross) * (-2.0 / width))


def identity(size):
    return (iota((size, size), 0) == iota((size, size), 1)).astype(jnp.float32)


def factor_step(work, j):
    lo, hi = 64 * j, 64 * j + 64
    inverse = factor64([work[lo:hi, lo:hi]])[0]
    rows = dot(inverse, work[lo:hi, :])
    work[lo:hi, :] = rows
    if j < 3:
        work[hi:, :] = work[hi:, :] - dot(rows[:, hi:256], rows, 0, 0)


def whole_body(
    pt_hbm, tt_hbm, ct_hbm, index_ref, index_hbm, out_ref,
    points, points2, targets, coefs, coefs2, index_rows, picked, landed, blocks,
    sums, from_x, from_y, from_z, sum_x, sum_y, total,
    work, link, hand, thin_in, solved,
    local_sem, send_sem, recv_sem, role_send, role_recv,
):
    y, x, c, z = spot()
    line = lax.axis_index("rows")
    me = line * NZ + z
    width, count = pt_hbm.shape
    classes = ct_hbm.shape[0]
    nblocks = index_ref.shape[0]
    mail = Mail(send_sem, recv_sem)

    greeted = greet()
    loads = [
        pltpu.make_async_copy(pt_hbm, points.at[pl.ds(0, width)], local_sem.at[0]),
        pltpu.make_async_copy(tt_hbm, targets, local_sem.at[1]),
        pltpu.make_async_copy(ct_hbm, coefs, local_sem.at[2]),
        pltpu.make_async_copy(index_hbm, index_rows, local_sem.at[3]),
    ]
    for load in loads:
        load.start()
    points[width:, :] = jnp.zeros((points.shape[0] - width, count), jnp.float32)
    points2[width:, :] = jnp.zeros((points.shape[0] - width, count), jnp.float32)
    row_no = iota((16, count), 0)
    mine = jnp.full((16, count), -1, jnp.int32)
    for k in range(nblocks):
        for i in range(PART):
            mine = jnp.where(row_no == PART * k + i, index_ref[k, line * PART + i], mine)
    owned = (mine == iota((16, count), 1) + me * count).astype(jnp.float32)
    for load in loads:
        load.wait()
    rows = dot(owned, points[...], 1, 1)
    for ch in range(CHUNKS):
        picked[ch] = rows[:, 128 * ch : 128 * ch + 128]
    start = dot(targets[...] - ridge * coefs[...], owned, 1, 1)
    sums[...] = jnp.zeros_like(sums)
    pick, lane = iota((16, 128), 0), iota((16, 128), 1)
    for k in range(nblocks):
        at = (pick // PART == k) & (lane == x * 32 + pick % PART * 8 + y)
        sums[CLASS_ROWS * k : CLASS_ROWS * k + classes, :] = -dot(start, at.astype(jnp.float32))
    pl.semaphore_wait(pltpu.get_barrier_semaphore(), greeted)

    k, i = z // PART, z % PART
    my_y = pl.ds(y, 1)
    step1 = [mail.send("z", s, picked.at[:, pl.ds((z + s) % NZ, 1)], landed.at[s]) for s in range(1, NZ)]
    pair = [mail.send("c", 1, points.at[pl.ds(0, width)], points2.at[pl.ds(0, width)])]
    pair.append(mail.send("c", 1, coefs, coefs2))
    arrive(step1)
    row = picked[:, pl.ds(z, 1), :]
    for s in range(1, NZ):
        row = row + landed[s]
    for ch in range(CHUNKS):
        blocks[c, ch, x, k, i, my_y, :] = row[ch]
    one = blocks.at[c, 0:3, x, k, i, my_y]
    ab1 = mail.spread("z", one, one)
    one = blocks.at[c, 3, x, k, i, my_y]
    c1 = mail.spread("x", one, one)
    arrive(c1)
    some = blocks.at[c, 3, :, k, i, my_y]
    c2 = mail.spread("y", some, some)
    arrive(ab1)
    some = blocks.at[c, 0:2, x, :, :, my_y]
    a2 = mail.spread("y", some, some)
    some = blocks.at[c, 2, x, :, :, my_y]
    b2 = mail.spread("x", some, some)
    arrive(c2)
    many = blocks.at[c, 3, :, k, i]
    c3 = mail.spread("z", many, many)
    arrive(b2)
    many = blocks.at[c, 2, :, :, :, my_y]
    b3 = mail.spread("y", many, many)
    arrive(a2)
    many = blocks.at[c, 0:2, x]
    a3 = mail.spread("x", many, many)
    arrive(pair)
    arrive(a3)
    arrive(b3)
    arrive(c3)
    other = [mail.send("c", 1, blocks.at[c], blocks.at[c])]

    half = jnp.concatenate([half_rows(blocks, c, k) for k in range(nblocks)], axis=0)
    term = dot(coefs[...], kernel_points(half, points[...], width), 1, 1)
    term = term + dot(coefs2[...], kernel_points(half, points2[...], width), 1, 1)
    for k in range(nblocks):
        at = slice(CLASS_ROWS * k, CLASS_ROWS * k + classes)
        sums[at, :] = sums[at, :] + term[:, 128 * k : 128 * k + 128]

    def tall_at(x):
        return pl.ds(pl.multiple_of(x * TALL, TALL), TALL)

    def low_at(y):
        return pl.ds(pl.multiple_of(y * LOW, LOW), LOW)

    sent = [mail.send("x", s, sums.at[tall_at((x + s) % NX)], from_x.at[s]) for s in range(1, NX)]
    role = z % ROLES
    arrive(other)
    own = whole_rows(blocks, role)
    work[:, 256:] = identity(256)
    work[:, :256] = kernel_block(own, own, width) + ridge * identity(256)
    factor_step(work, 0)
    arrive(sent)
    value = sums[tall_at(x)]
    for s in range(1, NX):
        value = value + from_x[s]
    sum_x[...] = value
    sent = [mail.send("y", s, sum_x.at[low_at((y + s) % NY)], from_y.at[s]) for s in range(1, NY)]
    factor_step(work, 1)
    arrive(sent)
    value = sum_x[low_at(y)]
    for s in range(1, NY):
        value = value + from_y[s]
    sum_y[...] = value
    sent = [mail.send("z", s, sum_y, from_z.at[s]) for s in range(1, NZ)]

    lane = iota((256, 256), 1)
    at = iota((256, 256), 0)
    line_of = (lane % 8 * NX + lane // 32 % 4) * NC + lane // 128
    order = (at == line_of * PART + lane // 8 % 4).astype(jnp.float32)
    numbers = dot(index_rows[...].astype(jnp.float32), order)

    def link_of(k, j):
        column = jnp.sum(jnp.where(at == lane, numbers[k : k + 1, :], 0.0), axis=1, keepdims=True)
        same = (column == numbers[j : j + 1, :]).astype(jnp.float32)
        return kernel_block(whole_rows(blocks, k), whole_rows(blocks, j), width) + ridge * same

    @pl.when(role == 2)
    def _():
        link[0] = link_of(2, 0)
        link[1] = link_of(2, 1)

    @pl.when(role == 1)
    def _():
        link[0] = link_of(1, 0)

    factor_step(work, 2)
    factor_step(work, 3)
    arrive(sent)
    for s in range(1, NZ):
        value = value + from_z[s]
    mine = pl.ds(pl.multiple_of(x * TALL + y * LOW, LOW), LOW)
    total[c, mine, :] = value
    sent = mail.spread("y", total.at[c, mine], total.at[c, mine])

    def role_copy(source, target, send, recv, to):
        return pltpu.make_async_remote_copy(
            src_ref=source, dst_ref=target, send_sem=role_send.at[send], recv_sem=role_recv.at[recv],
            device_id=device(y, x, c, z - role + to), device_id_type=MESH,
        )

    hands = {(2, 1): role_copy(hand.at[1], thin_in.at[0], 0, 0, 1),
             (2, 0): role_copy(hand.at[0], thin_in.at[1], 1, 1, 0),
             (1, 0): role_copy(hand.at[0], thin_in.at[2], 2, 2, 0)}
    gives = {(k, to): role_copy(solved.at[k], solved.at[k], 3 + 2 * k + n, 3 + k, to)
             for k in range(ROLES) for n, to in enumerate([t for t in range(ROLES) if t != k])}

    pick, lane = iota((16, 256), 0), iota((16, 256), 1)

    def solve(k, taken):
        at = (pick // PART == k) & (lane == c * 128 + x * 32 + pick % PART * 8 + y)
        value = at.astype(jnp.float32)
        for term in taken:
            value = value - term
        inverse = work[:, 256:]
        value = dot(dot(value, inverse, 1, 1), inverse)
        solved[k] = value
        return value

    def give(k):
        for to in range(ROLES):
            if to != k:
                gives[k, to].start()

    @pl.when(role == 2)
    def _():
        value = solve(2, [])
        hand[1] = dot(value, link[1])
        hands[2, 1].start()
        hand[0] = dot(value, link[0])
        hands[2, 0].start()
        give(2)

    @pl.when(role == 1)
    def _():
        hands[2, 1].wait_recv()
        value = solve(1, [thin_in[0]])
        hand[0] = dot(value, link[0])
        hands[1, 0].start()
        give(1)

    arrive(sent)
    sent = mail.spread("x", total.at[c, tall_at(x)], total.at[c, tall_at(x)])

    @pl.when(role == 0)
    def _():
        hands[2, 0].wait_recv()
        hands[1, 0].wait_recv()
        solve(0, [thin_in[1], thin_in[2]])
        give(0)

    arrive(sent)
    sent = [mail.send("c", 1, total.at[c], total.at[c])]
    for k in range(ROLES):

        @pl.when(role != k)
        def _():
            gives[k, (k + 1) % ROLES].wait_recv()

    arrive(sent)
    change = jnp.zeros((classes, 16), jnp.float32)
    for k in range(nblocks):
        for cc in range(NC):
            rows = total[cc, CLASS_ROWS * k : CLASS_ROWS * k + classes, :]
            change = change - dot(rows, solved[k, :, 128 * cc : 128 * cc + 128], 1, 1)
    out_ref[...] = coefs[...] + dot(change, owned)

    mail.close()

    @pl.when(role == 2)
    def _():
        hands[2, 1].wait_send()
        hands[2, 0].wait_send()

    @pl.when(role == 1)
    def _():
        hands[1, 0].wait_send()

    for k in range(ROLES):

        @pl.when(role == k)
        def _():
            for to in range(ROLES):
                if to != k:
                    gives[k, to].wait_send()


def body(points, targets, coefs, block_index):
    blocks, size = block_index.shape
    count, width = points.shape
    classes = targets.shape[1]
    f32 = jnp.float32
    out = pl.pallas_call(
        whole_body,
        out_shape=jax.ShapeDtypeStruct((classes, count), f32),
        in_specs=[ANY, ANY, ANY, SMEM, ANY],
        out_specs=VMEM,
        scratch_shapes=[
            pltpu.VMEM((128 * CHUNKS, count), f32),
            pltpu.VMEM((128 * CHUNKS, count), f32),
            pltpu.VMEM((classes, count), f32),
            pltpu.VMEM((classes, count), f32),
            pltpu.VMEM((classes, count), f32),
            pltpu.VMEM((blocks, size), jnp.int32),
            pltpu.VMEM((CHUNKS, 16, 128), f32),
            pltpu.VMEM((NZ, CHUNKS, 1, 128), f32),
            pltpu.VMEM((NC, CHUNKS, NX, blocks, PART, NY, 128), f32),
            pltpu.VMEM((PAD, 128), f32),
            pltpu.VMEM((NX, TALL, 128), f32),
            pltpu.VMEM((NY, LOW, 128), f32),
            pltpu.VMEM((NZ, LOW, 128), f32),
            pltpu.VMEM((TALL, 128), f32),
            pltpu.VMEM((LOW, 128), f32),
            pltpu.VMEM((NC, PAD, 128), f32),
            pltpu.VMEM((size, 2 * size), f32),
            pltpu.VMEM((2, size, size), f32),
            pltpu.VMEM((2, 16, size), f32),
            pltpu.VMEM((3, 16, size), f32),
            pltpu.VMEM((ROLES, 16, size), f32),
            pltpu.SemaphoreType.DMA((4,)),
            pltpu.SemaphoreType.DMA((COPIES,)),
            pltpu.SemaphoreType.DMA((COPIES,)),
            pltpu.SemaphoreType.DMA((9,)),
            pltpu.SemaphoreType.DMA((6,)),
        ],
        compiler_params=pltpu.CompilerParams(vmem_limit_bytes=56 << 20, collective_id=1, has_side_effects=True),
        name="block_updates",
    )(points.T, targets.T, coefs.T, block_index, block_index)
    return out.T


def solution(mesh):
    return jax.shard_map(
        body,
        mesh=mesh,
        in_specs=(
            P(("rows", "grp"), None),
            P(("rows", "grp"), None),
            P(("rows", "grp"), None),
            P(),
        ),
        out_specs=P(("rows", "grp"), None),
        check_vma=False,
    )
```

time: 1670 us -> 81.1 us (0.05)
  waiting for transfers between devices: 1150 us -> 0 us
  blocking collectives: 287 us -> 0 us
  other arithmetic: 171 us -> 0 us
  Pallas kernels: 0 us -> 79.3 us
  between operations: 25.4 us -> 0.01 us
  local copies, waits for them, and re-layouts: 23.4 us -> 1.59 us
    psum x3 -> x0, waiting for transfers between devices: 1150 us -> none  [body(): summed = lax.psum(partial_value, ('rows', 'grp'))]
    all_gather x3 -> x0, blocking collectives: 182 us -> none  [collect(): arrived = lax.all_gather(spread, 'rows', axis=0, tiled=True)]
    another operation x28 -> x0, other arithmetic: 163 us -> none  [the longest x21 104 us: solve_block(): factor = jnp.linalg.cholesky(system)]
    psum x3 -> x0, blocking collectives: 105 us -> none  [broadcast(): return lax.psum(block, axis)]
    pallas_call x0 -> x1, Pallas kernels: none -> 79.3 us  [body(): pl.pallas_call(whole_body, out_shape=jax.ShapeDtypeStruct((classes, count...]
  transfers between devices with their start and end apart: 3 -> 0, of which waited for: 3 -> 0; matrix products, arithmetic and copies ran while one was open for 11% -> 0% of each run, Pallas kernels for 0% -> 0%
where the time goes in v2:
time: 81.1 us; the launch traced here: 80.9 us
  Pallas kernels  79.3 us (98%)
  local copies, waits for them, and re-layouts  1.59 us (2%)
    pallas_call x1, Pallas kernels, body(): pl.pallas_call(whole_body, out_shape=jax.ShapeDtypeStruct((classes, count...  79.3 us

profile of v2, /device:TPU:1, one launch (start us, length us, event | category | flops | bytes accessed | tf_op | source)
XLA Modules:
  0.0 80.9 jit_solution(17448219240024274762)
XLA Ops:
  0.0 79.3 %block_updates.1 = f32[147,256]{1,0:T(8,128)} custom-call(f32[440,256]{1,0:T(8,128)} %bitcast.5, f32[147,256]{1,0:T(8,128)} %bitcast.6, f32[147,256]{1,0:T(8,128)} %bitcast.7, s32[3,256]{1,0:T(4,128)} %index_hbm.1, s32[3,256]{1,0:T(4,128)} %index_hbm.1), custom_call_target="tpu_custom_call" | custom-call | tf_op jit(solution)/shard_map/block_updates/pallas_call | solution.py:438
  79.3 1.6 %copy.6 = f32[256,147]{0,1:T(8,128)} copy(f32[256,147]{0,1:T(8,128)} %bitcast.4) | data formatting | bytes 301056

commit v3 on v2

v3 whole, which is shorter than its diff:
```python
import functools

import jax
import jax.numpy as jnp
from jax import lax
from jax.experimental import pallas as pl
from jax.experimental.pallas import tpu as pltpu
from jax.sharding import PartitionSpec as P

HIGH = lax.Precision.HIGHEST
VMEM = pl.BlockSpec(memory_space=pltpu.VMEM)
HBM = pl.BlockSpec(memory_space=pltpu.HBM)
MESH = pl.DeviceIdType.MESH
NY, NX, NC, NZ = 8, 4, 2, 12
PART = 4
CHUNKS = 4
PAD = 512
TALL, LOW = PAD // NX, PAD // NX // NY
CLASS_ROWS = 152
ROLES = 3
SPLIT = 3
ridge = 0.5


def dot(a, b, ca=1, cb=0):
    return lax.dot_general(a, b, (((ca,), (cb,)), ((), ())), precision=HIGH, preferred_element_type=jnp.float32)


def row_of(v, k):
    return jnp.broadcast_to(v[k:k + 1, :], v.shape)


def lane_of(v, k):
    return jnp.broadcast_to(v[:, k:k + 1], v.shape)


def eliminate(rows, t):
    place = lax.broadcasted_iota(jnp.int32, (8, 128), 0)
    top = rows[0]
    spread = [[lane_of(v, j) for j in range(8)] for v in rows[1:]]
    cols = [lane_of(top, j) for j in range(8)]
    forward = top
    full = top
    scale = jnp.zeros((8, 128), jnp.float32)
    for k in range(8):
        pivot = row_of(cols[k], k)
        inverse = 1.0 / pivot
        scale = jnp.where(place == k, inverse, scale)
        step = cols[k] * inverse
        both = jnp.where(place == k, 0.0, step)
        below = jnp.where(place > k, step, 0.0)
        for j in range(k + 1, 8):
            cols[j] = cols[j] - both * row_of(cols[j], k)
        forward = forward - below * row_of(forward, k)
        full = full - both * row_of(full, k)
    solved = full * scale
    done = forward * jnp.sqrt(scale)
    lines = [row_of(solved, j) for j in range(8)]
    out = []
    for p in range(1, 8):
        s = spread[p - 1]
        terms = [s[j] * lines[j] for j in range(8)]
        total = ((terms[0] + terms[1]) + (terms[2] + terms[3])) + ((terms[4] + terms[5]) + (terms[6] + terms[7]))
        live = jnp.where(t + p < 8, 1.0, 0.0).astype(jnp.float32)
        out.append(rows[p] - live * total)
    out.append(done)
    return [pltpu.roll(v, 120, 1) for v in out]


def factor_start(work, j):
    lo, hi = 64 * j, 64 * j + 64
    wide = jnp.concatenate([work[lo:hi, lo:hi], identity(64)], axis=1)
    return tuple(wide[8 * p : 8 * p + 8, :] for p in range(8))


def factor_groups(state, first, last):
    return lax.fori_loop(first, last, lambda t, state: tuple(eliminate(list(state), t)), state)


def factor_end(work, j, state):
    lo, hi = 64 * j, 64 * j + 64
    inverse = jnp.concatenate(state, axis=0)[:, :64]
    rows = dot(inverse, work[lo:hi, :])
    work[lo:hi, :] = rows
    if j < 3:
        work[hi:, :] = work[hi:, :] - dot(rows[:, hi:256], rows, 0, 0)


def iota(shape, axis):
    return lax.broadcasted_iota(jnp.int32, shape, axis)


def spot():
    line = lax.axis_index("rows")
    return line // (NX * NC), line // NC % NX, line % NC, lax.axis_index("grp")


def device(y, x, c, z):
    return ((y * NX + x) * NC + c, z)


def partner(axis, step):
    y, x, c, z = spot()
    if axis == "y":
        return device((y + step) % NY, x, c, z)
    if axis == "x":
        return device(y, (x + step) % NX, c, z)
    if axis == "z":
        return device(y, x, c, (z + step) % NZ)
    return device(y, x, (c + step) % NC, z)


SIZES = {"y": NY, "x": NX, "z": NZ, "c": NC}


def far_first(size):
    return sorted(range(1, size), key=lambda step: -min(step, size - step))


def greet():
    barrier = pltpu.get_barrier_semaphore()
    count = 0
    for axis, size in SIZES.items():
        for step in range(1, size):
            pl.semaphore_signal(barrier, inc=1, device_id=partner(axis, step), device_id_type=MESH)
            count += 1
    return count


class Mail:
    def __init__(self, send_sem, recv_sem):
        self.send_sem, self.recv_sem, self.used, self.sent = send_sem, recv_sem, 0, []

    def send(self, axis, step, source, target):
        copy = pltpu.make_async_remote_copy(
            src_ref=source,
            dst_ref=target,
            send_sem=self.send_sem.at[self.used],
            recv_sem=self.recv_sem.at[self.used],
            device_id=partner(axis, step),
            device_id_type=MESH,
        )
        copy.start()
        self.used += 1
        self.sent.append(copy)
        return copy

    def spread(self, axis, source, target):
        return [self.send(axis, step, source, target) for step in far_first(SIZES[axis])]

    def close(self):
        for copy in self.sent:
            copy.wait_send()


def arrive(copies):
    for copy in copies:
        copy.wait_recv()


COPIES = (
    2 + 2 * (NZ - 1) + 3 * (NX - 1 + NY - 1) + 1
    + (NX - 1) + (NY - 1) + (NZ - 1) + (NY - 1) + NY * (NX - 1) + NX
)


def half_rows(blocks_ref, c, k, lo=0, hi=CHUNKS):
    return jnp.concatenate([blocks_ref[c, ch, :, k].reshape(-1, 128) for ch in range(lo, hi)], axis=1)


def whole_rows(blocks_ref, k):
    return jnp.concatenate([half_rows(blocks_ref, c, k) for c in range(NC)], axis=0)


def kernel_block(left, right, width):
    cross = dot(left, right, 1, 1)
    left_sq = jnp.sum(left * left, axis=1, keepdims=True)
    right_sq = dot(jnp.ones((8, right.shape[1]), jnp.float32), right * right, 1, 1)[:1]
    return jnp.exp((left_sq + right_sq - 2.0 * cross) * (-2.0 / width))


def identity(size):
    return (iota((size, size), 0) == iota((size, size), 1)).astype(jnp.float32)


def factor_step(work, j):
    factor_end(work, j, factor_groups(factor_start(work, j), 0, 8))


def whole_body(
    pt_hbm, tt_hbm, ct_hbm, index_hbm, out_ref,
    index_ref, points, targets, coefs, index_rows, picked, landed, blocks,
    far, sums, from_x, from_y, from_z, sum_x, sum_y, total,
    work, link, solved,
    local_sem, send_sem, recv_sem, role_send, role_recv,
):
    y, x, c, z = spot()
    line = lax.axis_index("rows")
    me = line * NZ + z
    width, count = pt_hbm.shape
    classes = ct_hbm.shape[0]
    nblocks = index_hbm.shape[0]
    mail = Mail(send_sem, recv_sem)

    greeted = greet()
    loads = [
        pltpu.make_async_copy(index_hbm, index_ref, local_sem.at[0]),
        pltpu.make_async_copy(pt_hbm, points.at[pl.ds(0, width), pl.ds(0, count)], local_sem.at[1]),
        pltpu.make_async_copy(ct_hbm, coefs.at[:, pl.ds(0, count)], local_sem.at[2]),
        pltpu.make_async_copy(tt_hbm, targets, local_sem.at[3]),
        pltpu.make_async_copy(index_hbm, index_rows, local_sem.at[4]),
    ]
    for load in loads:
        load.start()
    points[width:, :] = jnp.zeros((points.shape[0] - width, 2 * count), jnp.float32)
    row_no = iota((16, count), 0)
    mine = jnp.full((16, count), -1, jnp.int32)
    loads[0].wait()
    for k in range(nblocks):
        for i in range(PART):
            mine = jnp.where(row_no == PART * k + i, index_ref[k, line * PART + i], mine)
    owned = (mine == iota((16, count), 1) + me * count).astype(jnp.float32)
    loads[1].wait()
    rows = dot(owned, points[:, :count], 1, 1)
    for ch in range(CHUNKS):
        picked[ch] = rows[:, 128 * ch : 128 * ch + 128]
    pl.semaphore_wait(pltpu.get_barrier_semaphore(), greeted)

    my_y = pl.ds(y, 1)
    first = [mail.send("z", s, picked.at[:, pl.ds((z + s) % NZ, 1)], landed.at[s]) for s in far_first(NZ)]
    loads[2].wait()
    pair = [mail.send("c", 1, points.at[pl.ds(0, width), pl.ds(0, count)], points.at[pl.ds(0, width), pl.ds(count, count)])]
    pair.append(mail.send("c", 1, coefs.at[:, pl.ds(0, count)], coefs.at[:, pl.ds(count, count)]))
    loads[3].wait()
    loads[4].wait()

    start = dot(targets[...] - ridge * coefs[:, :count], owned, 1, 1)
    sums[...] = jnp.zeros_like(sums)
    pick, lane = iota((16, 128), 0), iota((16, 128), 1)
    for k in range(nblocks):
        at = (pick // PART == k) & (lane == x * 32 + pick % PART * 8 + y)
        sums[CLASS_ROWS * k : CLASS_ROWS * k + classes, :] = -dot(start, at.astype(jnp.float32))

    arrive(first)
    row = picked[:, pl.ds(z, 1), :]
    for s in range(1, NZ):
        row = row + landed[s]
    my_k, my_i = z // PART, z % PART
    for ch in range(CHUNKS):
        blocks[c, ch, x, my_k, my_i, my_y, :] = row[ch]
    one = blocks.at[c, :, x, my_k, my_i, my_y]
    arrive(mail.spread("z", one, one))

    def along_y(lo, hi):
        some = blocks.at[c, lo:hi, x, :, :, my_y]
        return mail.spread("y", some, some)

    y0 = along_y(0, 2)
    some = blocks.at[c, 2, x, :, :, my_y]
    x1 = mail.spread("x", some, some)
    y2 = along_y(3, 4)
    arrive(x1)
    many = blocks.at[c, 2, :, :, :, my_y]
    y1 = mail.spread("y", many, many)
    arrive(y0)
    many = blocks.at[c, 0:2, x]
    x0 = mail.spread("x", many, many)
    arrive(y2)
    many = blocks.at[c, 3, x]
    x2 = mail.spread("x", many, many)

    arrive(pair)
    points_sq = jnp.sum(points[...] * points[...], axis=0, keepdims=True)

    def cross_part(lo):
        half = jnp.concatenate([half_rows(blocks, c, k, lo, lo + 2) for k in range(nblocks)], axis=0)
        squares = jnp.sum(half * half, axis=1, keepdims=True)
        return squares - 2.0 * dot(half, points[128 * lo : 128 * lo + 256, :])

    arrive(x0)
    far[...] = cross_part(0) + points_sq
    arrive(y1)
    arrive(x2)
    other = [mail.send("c", 1, blocks.at[c], blocks.at[c])]
    kern = jnp.exp((far[...] + cross_part(2)) * (-2.0 / width))
    term = dot(coefs[...], kern, 1, 1)
    for k in range(nblocks):
        at = slice(CLASS_ROWS * k, CLASS_ROWS * k + classes)
        sums[at, :] = sums[at, :] + term[:, 128 * k : 128 * k + 128]

    def tall_at(x):
        return pl.ds(pl.multiple_of(x * TALL, TALL), TALL)

    def low_at(y):
        return pl.ds(pl.multiple_of(y * LOW, LOW), LOW)

    sent = [mail.send("x", s, sums.at[tall_at((x + s) % NX)], from_x.at[s]) for s in far_first(NX)]
    role = z % ROLES
    arrive(other)
    own = whole_rows(blocks, role)
    work[:, 256:] = identity(256)
    work[:, :256] = kernel_block(own, own, width) + ridge * identity(256)
    state = factor_groups(factor_start(work, 0), 0, SPLIT)
    arrive(sent)
    value = sums[tall_at(x)]
    for s in range(1, NX):
        value = value + from_x[s]
    sum_x[...] = value
    sent = [mail.send("y", s, sum_x.at[low_at((y + s) % NY)], from_y.at[s]) for s in far_first(NY)]
    factor_end(work, 0, factor_groups(state, SPLIT, 8))
    factor_step(work, 1)
    arrive(sent)
    value = sum_x[low_at(y)]
    for s in range(1, NY):
        value = value + from_y[s]
    sum_y[...] = value
    sent = [mail.send("z", s, sum_y, from_z.at[s]) for s in far_first(NZ)]

    factor_step(work, 2)
    factor_step(work, 3)
    arrive(sent)
    for s in range(1, NZ):
        value = value + from_z[s]
    def piece_of(y):
        return total.at[c, pl.ds(pl.multiple_of(x * TALL + y * LOW, LOW), LOW)]

    mine = piece_of(y)
    mine[...] = value
    down = {s: mail.send("y", s, mine, mine) for s in far_first(NY)}
    across = mail.spread("x", mine, mine)

    gives = {}
    for k in range(ROLES):
        for n, to in enumerate([to for to in range(ROLES) if to != k]):
            gives[k, to] = pltpu.make_async_remote_copy(
                src_ref=solved.at[k],
                dst_ref=solved.at[k],
                send_sem=role_send.at[2 * k + n],
                recv_sem=role_recv.at[k],
                device_id=device(y, x, c, z - role + to),
                device_id_type=MESH,
            )

    def give(k):
        for to in range(ROLES):
            if to != k:
                gives[k, to].start()

    def through(value):
        inverse = work[:, 256:]
        return dot(dot(value, inverse, 1, 1), inverse)

    def own_pick(k):
        pick, lane = iota((16, 256), 0), iota((16, 256), 1)
        at = (pick // PART == k) & (lane == c * 128 + x * 32 + pick % PART * 8 + y)
        return at.astype(jnp.float32)

    def links(j):
        lane, at = iota((256, 256), 1), iota((256, 256), 0)
        line_of = (lane % 8 * NX + lane // 32 % 4) * NC + lane // 128
        order = (at == line_of * PART + lane // 8 % 4).astype(jnp.float32)
        numbers = dot(index_rows[...].astype(jnp.float32), order)
        for n, k in enumerate(range(j + 1, nblocks)):
            column = jnp.sum(jnp.where(at == lane, numbers[k : k + 1, :], 0.0), axis=1, keepdims=True)
            same = (column == numbers[j : j + 1, :]).astype(jnp.float32)
            link[n] = kernel_block(whole_rows(blocks, k), whole_rows(blocks, j), width) + ridge * same

    @pl.when(role == 2)
    def _():
        solved[2] = through(own_pick(2))
        give(2)

    @pl.when(role == 1)
    def _():
        links(1)
        link[0] = through(link[0])
        solved[1] = through(own_pick(1))

    @pl.when(role == 0)
    def _():
        links(0)

    def forward(s):
        arrive([down[s]])
        piece = piece_of((y - s + NY) % NY)
        return mail.spread("x", piece, piece)

    near_first = list(reversed(far_first(NY)))
    for s in near_first[:4]:
        across += forward(s)

    @pl.when(role == 1)
    def _():
        gives[2, 1].wait_recv()
        solved[1] = solved[1] - dot(solved[2], link[0])
        give(1)

    for s in near_first[4:]:
        across += forward(s)

    @pl.when(role == 0)
    def _():
        gives[2, 0].wait_recv()
        value = own_pick(0) - dot(solved[2], link[1])
        gives[1, 0].wait_recv()
        solved[0] = through(value - dot(solved[1], link[0]))
        give(0)

    tall = total.at[c, tall_at(x)]
    sent = [mail.send("c", 1, tall, tall)]

    arrive(across)
    for s in range(1, NX):
        tall = total.at[c, tall_at((x + s) % NX)]
        sent.append(mail.send("c", 1, tall, tall))
    @pl.when(role == 2)
    def _():
        gives[1, 2].wait_recv()

    @pl.when(role != 0)
    def _():
        gives[0, 1].wait_recv()

    def change_of(cc):
        change = jnp.zeros((classes, 16), jnp.float32)
        for k in range(nblocks):
            rows = total[cc, CLASS_ROWS * k : CLASS_ROWS * k + classes, :]
            at = pl.ds(pl.multiple_of(cc * 128, 128), 128)
            change = change - dot(rows, solved[k, :, at], 1, 1)
        return change

    change = change_of(c)
    arrive(sent)
    change = change + change_of(1 - c)
    out_ref[...] = coefs[:, :count] + dot(change, owned)

    mail.close()

    for k in range(ROLES):

        @pl.when(role == k)
        def _():
            for to in range(ROLES):
                if to != k:
                    gives[k, to].wait_send()


def body(points, targets, coefs, block_index):
    blocks, size = block_index.shape
    count, width = points.shape
    classes = targets.shape[1]
    f32 = jnp.float32
    out = pl.pallas_call(
        whole_body,
        out_shape=jax.ShapeDtypeStruct((classes, count), f32),
        in_specs=[HBM] * 4,
        out_specs=VMEM,
        scratch_shapes=[
            pltpu.SMEM((blocks, size), jnp.int32),
            pltpu.VMEM((128 * CHUNKS, 2 * count), f32),
            pltpu.VMEM((classes, count), f32),
            pltpu.VMEM((classes, 2 * count), f32),
            pltpu.VMEM((blocks, size), jnp.int32),
            pltpu.VMEM((CHUNKS, 16, 128), f32),
            pltpu.VMEM((NZ, CHUNKS, 1, 128), f32),
            pltpu.VMEM((NC, CHUNKS, NX, blocks, PART, NY, 128), f32),
            pltpu.VMEM((blocks * size // 2, 2 * count), f32),
            pltpu.VMEM((PAD, 128), f32),
            pltpu.VMEM((NX, TALL, 128), f32),
            pltpu.VMEM((NY, LOW, 128), f32),
            pltpu.VMEM((NZ, LOW, 128), f32),
            pltpu.VMEM((TALL, 128), f32),
            pltpu.VMEM((LOW, 128), f32),
            pltpu.VMEM((NC, PAD, 128), f32),
            pltpu.VMEM((size, 2 * size), f32),
            pltpu.VMEM((2, size, size), f32),
            pltpu.VMEM((ROLES, 16, size), f32),
            pltpu.SemaphoreType.DMA((5,)),
            pltpu.SemaphoreType.DMA((COPIES,)),
            pltpu.SemaphoreType.DMA((COPIES,)),
            pltpu.SemaphoreType.DMA((2 * ROLES,)),
            pltpu.SemaphoreType.DMA((ROLES,)),
        ],
        compiler_params=pltpu.CompilerParams(vmem_limit_bytes=56307712, collective_id=1, has_side_effects=True),
        name="block_updates",
    )(points.T, targets.T, coefs.T, block_index)
    return out.T


def solution(mesh):
    return jax.shard_map(
        body,
        mesh=mesh,
        in_specs=(
            P(("rows", "grp"), None),
            P(("rows", "grp"), None),
            P(("rows", "grp"), None),
            P(),
        ),
        out_specs=P(("rows", "grp"), None),
        check_vma=False,
    )
```

time: 81.1 us -> 75.9 us (0.936)
  Pallas kernels: 79.3 us -> 74.4 us
    pallas_call x1, Pallas kernels: 79.3 us -> 74.4 us  [body(): pl.pallas_call(whole_body, out_shape=jax.ShapeDtypeStruct((classes, count...]
where the time goes in v3:
time: 75.9 us; the launch traced here: 75.7 us
  Pallas kernels  74.4 us (98%)
  local copies, waits for them, and re-layouts  1.35 us (2%)
    pallas_call x1, Pallas kernels, body(): pl.pallas_call(whole_body, out_shape=jax.ShapeDtypeStruct((classes, count...  74.4 us

profile of v3, /device:TPU:1, one launch (start us, length us, event | category | flops | bytes accessed | tf_op | source)
XLA Modules:
  0.0 75.7 jit_solution(418774344449333398)
XLA Ops:
  0.0 0.0 copy-start
  0.0 0.7 copy-done
  0.7 74.4 %block_updates.1 = f32[147,256]{1,0:T(8,128)S(1)} custom-call(f32[440,256]{1,0:T(8,128)} %bitcast.5, f32[147,256]{1,0:T(8,128)} %bitcast.6, f32[147,256]{1,0:T(8,128)} %bitcast.7, s32[3,256]{1,0:T(4,128)S(1)} %copy-done), custom_call_target="tpu_custom_call" | custom-call | tf_op jit(solution)/shard_map/block_updates/pallas_call | solution.py:453
  75.1 0.7 copy.6
Async XLA Ops:
  0.0 0.7 copy-start

commit v4 on v3

--- a/solution.py
+++ b/solution.py
@@ -14,9 +14,9 @@
 NY, NX, NC, NZ = 8, 4, 2, 12
 PART = 4
 CHUNKS = 4
-PAD = 512
+PAD = 448
 TALL, LOW = PAD // NX, PAD // NX // NY
-CLASS_ROWS = 152
+CLASS_ROWS = 147
 ROLES = 3
 SPLIT = 3
 ridge = 0.5
@@ -256,18 +256,14 @@
         return mail.spread("y", some, some)
 
     y0 = along_y(0, 2)
-    some = blocks.at[c, 2, x, :, :, my_y]
+    some = blocks.at[c, 2:4, x, :, :, my_y]
     x1 = mail.spread("x", some, some)
-    y2 = along_y(3, 4)
     arrive(x1)
-    many = blocks.at[c, 2, :, :, :, my_y]
+    many = blocks.at[c, 2:4, :, :, :, my_y]
     y1 = mail.spread("y", many, many)
     arrive(y0)
     many = blocks.at[c, 0:2, x]
     x0 = mail.spread("x", many, many)
-    arrive(y2)
-    many = blocks.at[c, 3, x]
-    x2 = mail.spread("x", many, many)
 
     arrive(pair)
     points_sq = jnp.sum(points[...] * points[...], axis=0, keepdims=True)
@@ -280,7 +276,6 @@
     arrive(x0)
     far[...] = cross_part(0) + points_sq
     arrive(y1)
-    arrive(x2)
     other = [mail.send("c", 1, blocks.at[c], blocks.at[c])]
     kern = jnp.exp((far[...] + cross_part(2)) * (-2.0 / width))
     term = dot(coefs[...], kern, 1, 1)
@@ -409,9 +404,10 @@
     tall = total.at[c, tall_at(x)]
     sent = [mail.send("c", 1, tall, tall)]
 
-    arrive(across)
-    for s in range(1, NX):
-        tall = total.at[c, tall_at((x + s) % NX)]
+    near = list(reversed(far_first(NX)))
+    for n, s in enumerate(near):
+        arrive(across[len(near) - 1 - n :: len(near)])
+        tall = total.at[c, tall_at((x - s + NX) % NX)]
         sent.append(mail.send("c", 1, tall, tall))
     @pl.when(role == 2)
     def _():

time: 75.9 us -> 75.1 us (0.989)
  Pallas kernels: 74.4 us -> 73.6 us
    pallas_call x1, Pallas kernels: 74.4 us -> 73.6 us  [body(): pl.pallas_call(whole_body, out_shape=jax.ShapeDtypeStruct((classes, count...]
where the time goes in v4:
time: 75.1 us; the launch traced here: 74.9 us
  Pallas kernels  73.6 us (98%)
  local copies, waits for them, and re-layouts  1.35 us (2%)
    pallas_call x1, Pallas kernels, body(): pl.pallas_call(whole_body, out_shape=jax.ShapeDtypeStruct((classes, count...  73.6 us

profile of v4, /device:TPU:1, one launch (start us, length us, event | category | flops | bytes accessed | tf_op | source)
XLA Modules:
  0.0 74.9 jit_solution(17493547460850455181)
XLA Ops:
  0.0 0.0 copy-start
  0.0 0.7 copy-done
  0.7 73.6 %block_updates.1 = f32[147,256]{1,0:T(8,128)S(1)} custom-call(f32[440,256]{1,0:T(8,128)} %bitcast.5, f32[147,256]{1,0:T(8,128)} %bitcast.6, f32[147,256]{1,0:T(8,128)} %bitcast.7, s32[3,256]{1,0:T(4,128)S(1)} %copy-done), custom_call_target="tpu_custom_call" | custom-call | tf_op jit(solution)/shard_map/block_updates/pallas_call | solution.py:449
  74.3 0.7 copy.6
Async XLA Ops:
  0.0 0.7 copy-start

commit v5 on v4

--- a/solution.py
+++ b/solution.py
@@ -110,7 +110,7 @@
     return device(y, x, (c + step) % NC, z)
 
 
-SIZES = {"y": NY, "x": NX, "z": NZ, "c": NC}
+SIZES = {"z": NZ, "y": NY, "x": NX, "c": NC}
 
 
 def far_first(size):
@@ -121,7 +121,7 @@
     barrier = pltpu.get_barrier_semaphore()
     count = 0
     for axis, size in SIZES.items():
-        for step in range(1, size):
+        for step in far_first(size):
             pl.semaphore_signal(barrier, inc=1, device_id=partner(axis, step), device_id_type=MESH)
             count += 1
     return count

time: 75.1 us -> 75 us (level)
  no operation moved by 1% of the time
where the time goes in v5:
time: 75 us; the launch traced here: 74.8 us
  Pallas kernels  73.5 us (98%)
  local copies, waits for them, and re-layouts  1.35 us (2%)
    pallas_call x1, Pallas kernels, body(): pl.pallas_call(whole_body, out_shape=jax.ShapeDtypeStruct((classes, count...  73.5 us

profile of v5, /device:TPU:1, one launch (start us, length us, event | category | flops | bytes accessed | tf_op | source)
XLA Modules:
  0.0 74.8 jit_solution(14071837724472574606)
XLA Ops:
  0.0 0.0 copy-start
  0.0 0.7 copy-done
  0.7 73.5 %block_updates.1 = f32[147,256]{1,0:T(8,128)S(1)} custom-call(f32[440,256]{1,0:T(8,128)} %bitcast.5, f32[147,256]{1,0:T(8,128)} %bitcast.6, f32[147,256]{1,0:T(8,128)} %bitcast.7, s32[3,256]{1,0:T(4,128)S(1)} %copy-done), custom_call_target="tpu_custom_call" | custom-call | tf_op jit(solution)/shard_map/block_updates/pallas_call | solution.py:449
  74.2 0.7 copy.6
Async XLA Ops:
  0.0 0.7 copy-start
